TPU v7x, 32 devices: a whole 2x2x4 slice. The times are simulated.
32 devices in a mesh: seq: 16 (over z, y, x), head: 2 (over core).
Axes of the slice: x: 2, y: 2, z: 4, core: 2. Of those that a mesh axis runs over, the one named last changes fastest.
Arguments:
- q_lin: bfloat16 [4096, 512], P('seq', 'head'), may hold values from -6 to 6
- k_lin: bfloat16 [4096, 512], P('seq', 'head'), may hold values from -6 to 6
- v_lin: bfloat16 [4096, 512], P('seq', 'head'), may hold values from -6 to 6
- log_decay: float32 [4, 4096], P('head', 'seq'), may hold values from -0.4 to 0, as said below
- q_soft: bfloat16 [4096, 512], P('seq', 'head'), may hold values from -12 to 12
- k_soft: bfloat16 [4096, 512], P('seq', 'head'), may hold values from -6 to 6
- v_soft: bfloat16 [4096, 512], P('seq', 'head'), may hold values from -6 to 6
- wo_lin: bfloat16 [512, 4096], P('head'), may hold values from -0.375 to 0.375
- wo_soft: bfloat16 [512, 4096], P('head'), may hold values from -0.375 to 0.375
Outputs:
- lin_mixed: bfloat16 [4096, 4096], P('seq', 'head')
- soft_mixed: bfloat16 [4096, 4096], P('seq', 'head')
Inputs may be any that keep to these rules, and one draw needn't show every extreme that they name: `log_decay`: log decays are never positive.
All inputs are finite; a program needn't handle non-finite values.
Results may differ from a plain program's by a relative error of at most 0.012.
Values may be sent and summed in bfloat16 or wider, within the bound.
A program may use at most 64 MiB of HBM per device.

v0:
```python
import math

import jax
import jax.numpy as jnp
from jax import lax
from jax.sharding import PartitionSpec as P

HIGHEST = lax.Precision.HIGHEST
NEG_BIG = -1e30


def prefix(shard, axis, combine, identity):
    size, here = (lax.axis_size(axis), lax.axis_index(axis))
    everything = jax.tree.map(
        lambda part, kind: lax.all_gather(part.astype(kind), axis),
        shard,
        (jnp.bfloat16, jnp.bfloat16),
    )
    start = jax.tree.map(
        lambda part, zero: jnp.broadcast_to(jnp.asarray(zero, part.dtype), part.shape),
        shard,
        identity,
    )

    def turn(k, before):
        reached = k < here
        new = combine(
            before, jax.tree.map(lambda part, own: part[k].astype(own.dtype), everything, shard)
        )
        return jax.tree.map(lambda a, b: jnp.where(reached, a, b), new, before)

    return lax.fori_loop(0, size, turn, start)


def second_half(device):
    return 2 * device + 1


def absorb(state, query_half, key_block, value_block, allowed, factor):
    row_top, row_sum, weighted = state
    scores = (
        jnp.einsum("qhd,khd->hqk", query_half, key_block, preferred_element_type=jnp.float32)
        * factor
    )
    if allowed is not None:
        scores = jnp.where(allowed[None], scores, -jnp.inf)
    new_top = jnp.maximum(row_top, jnp.max(scores, axis=-1))
    shrink = jnp.exp(row_top - new_top)
    weights = jnp.exp(scores - new_top[:, :, None])
    row_sum = row_sum * shrink + jnp.sum(weights, axis=-1)
    weighted = weighted * shrink.T[:, :, None] + jnp.einsum(
        "hqk,khd->qhd",
        weights.astype(jnp.bfloat16),
        value_block,
        preferred_element_type=jnp.float32,
    )
    return (new_top, row_sum, weighted)


def lightning_heads(q_lin, k_lin, v_lin, log_decay):
    row_count = q_lin.shape[0]
    head_count = log_decay.shape[0]
    head_width = q_lin.shape[1] // head_count
    query_plain = q_lin.reshape(row_count, head_count, head_width)
    key_plain = k_lin.reshape(row_count, head_count, head_width)
    queries = query_plain.astype(jnp.float32)
    key_rows = key_plain.astype(jnp.float32)
    values = v_lin.astype(jnp.float32).reshape(row_count, head_count, head_width)
    cumulative = jnp.cumsum(log_decay, axis=1)
    lower = jnp.arange(row_count)[:, None] >= jnp.arange(row_count)[None, :]
    decay_gap = jnp.where(lower[None], cumulative[:, :, None] - cumulative[:, None, :], -jnp.inf)
    scores = jnp.einsum(
        "thd,shd->hts", query_plain, key_plain, preferred_element_type=jnp.float32
    ) * jnp.exp(decay_gap)
    inside = jnp.einsum("hts,shd->thd", scores, values, precision=HIGHEST)
    closing = jnp.exp(cumulative[:, -1:] - cumulative)
    own_state = jnp.einsum(
        "shd,she->hde", key_rows * closing.T[:, :, None], values, precision=HIGHEST
    )
    own_decay = cumulative[:, -1]

    def combine(earlier, later):
        return (jnp.exp(later[1])[:, None, None] * earlier[0] + later[0], earlier[1] + later[1])

    identity = (jnp.zeros_like(own_state), jnp.zeros_like(own_decay))
    carried, _ = prefix((own_state, own_decay), "seq", combine, identity)
    from_before = (
        jnp.einsum("thd,hde->the", queries, carried, precision=HIGHEST)
        * jnp.exp(cumulative).T[:, :, None]
    )
    raw = inside + from_before
    factor = lax.rsqrt(jnp.mean(raw * raw, axis=-1, keepdims=True) + 1e-06)
    return (raw * factor).astype(jnp.bfloat16).reshape(row_count, head_count * head_width)


def softmax_heads(q_soft, k_soft, v_soft, head_width):
    row_count = q_soft.shape[0]
    half_rows = row_count // 2
    head_count = q_soft.shape[1] // head_width
    own_index = lax.axis_index("seq")
    factor = 1.0 / math.sqrt(head_width)
    shaped = q_soft.reshape(2, half_rows, head_count, head_width)
    query_ids = (2 * own_index, second_half(own_index))
    triangle = jnp.arange(half_rows)[:, None] >= jnp.arange(half_rows)[None, :]

    def block_pass(state, side, key_block, value_block, key_id):

        def full_block(inner_state):
            return absorb(inner_state, shaped[side], key_block, value_block, None, factor)

        def diagonal_block(inner_state):
            return absorb(inner_state, shaped[side], key_block, value_block, triangle, factor)

        def skipped(inner_state):
            return inner_state

        def not_below(inner_state):
            return lax.cond(key_id == query_ids[side], diagonal_block, skipped, inner_state)

        return lax.cond(key_id < query_ids[side], full_block, not_below, state)

    start_state = tuple(
        (
            (
                jnp.full((head_count, half_rows), NEG_BIG, jnp.float32),
                jnp.zeros((head_count, half_rows), jnp.float32),
                jnp.zeros((half_rows, head_count, head_width), jnp.float32),
            )
            for side in range(2)
        )
    )
    carry = start_state
    key_piece = lax.all_gather(k_soft, "seq", axis=0, tiled=True)
    value_piece = lax.all_gather(v_soft, "seq", axis=0, tiled=True)
    piece_rows = key_piece.shape[0]
    blocks = piece_rows // half_rows
    key_blocks = key_piece.reshape(blocks, half_rows, head_count, head_width)
    value_blocks = value_piece.reshape(blocks, half_rows, head_count, head_width)
    firsts = half_rows * jnp.arange(blocks, dtype=jnp.int32)

    def inner(state, block_item):
        key_block, value_block, first = block_item
        key_id = first // half_rows
        return (
            tuple(
                (block_pass(state[side], side, key_block, value_block, key_id) for side in range(2))
            ),
            None,
        )

    carry, _ = lax.scan(inner, carry, (key_blocks, value_blocks, firsts))
    halves = [
        (carry[side][2] / carry[side][1].T[:, :, None])
        .astype(jnp.bfloat16)
        .reshape(half_rows, head_count * head_width)
        for side in range(2)
    ]
    return jnp.concatenate(halves, axis=0)


def local(q_lin, k_lin, v_lin, log_decay, q_soft, k_soft, v_soft, wo_lin, wo_soft):
    head_width = q_lin.shape[1] // log_decay.shape[0]
    lin_out = lightning_heads(q_lin, k_lin, v_lin, log_decay)
    soft_out = softmax_heads(q_soft, k_soft, v_soft, head_width)
    lin_term = jnp.dot(lin_out, wo_lin, preferred_element_type=jnp.float32)
    soft_term = jnp.dot(soft_out, wo_soft, preferred_element_type=jnp.float32)
    lin_sum, soft_sum = (
        lax.psum_scatter(
            lin_term.astype(jnp.bfloat16).astype(jnp.float32).astype(jnp.bfloat16),
            "head",
            scatter_dimension=1,
            tiled=True,
        ).astype(jnp.float32),
        lax.psum_scatter(
            soft_term.astype(jnp.bfloat16).astype(jnp.float32).astype(jnp.bfloat16),
            "head",
            scatter_dimension=1,
            tiled=True,
        ).astype(jnp.float32),
    )
    return (lin_sum.astype(jnp.bfloat16), soft_sum.astype(jnp.bfloat16))


def solution(mesh):
    in_specs = (
        P("seq", "head"),
        P("seq", "head"),
        P("seq", "head"),
        P("head", "seq"),
        P("seq", "head"),
        P("seq", "head"),
        P("seq", "head"),
        P("head", None),
        P("head", None),
    )
    out_specs = (P("seq", "head"), P("seq", "head"))
    return jax.shard_map(local, mesh=mesh, in_specs=in_specs, out_specs=out_specs, check_vma=False)
```

profile of v0, /device:TPU:25, one launch (start us, length us, event | category | flops | bytes accessed | tf_op | source)
XLA Modules:
  0.0 388.1 jit_solution(17133437121583700277)
XLA Ops:
  9.3 1.0 copy.69
  10.4 1.8 convolution_convert_fusion.2
  13.8 1.2 dynamic-slice
  15.9 27.0 %all-reduce = bf16[32]{0:T(256)(128)(2,1)S(1)} all-reduce(bf16[32]{0:T(256)(128)(2,1)S(1)} %dynamic-update-slice), channel_id=2, replica_groups=mesh['seq'=16,'head'=2] {'seq'}, use_global_device_ids=true, to_apply=%add | all-reduce | flops 32 | bytes 128
  43.9 1.1 convolution_multiply_fusion.4
  45.1 21.1 %all-gather.10.cloned.1.call-done = bf16[32,128,128]{2,1,0:T(8,128)(2,1)} async-done(((bf16[2,128,128]{2,1,0:T(8,128)(2,1)}), bf16[32,128,128]{2,1,0:T(8,128)(2,1)}) %all-gather.10.cloned.1.call-update) | async-done | bytes 1048592 | tf_op jit(solution)/shard_map/all_gather | solution.py:15
  66.2 15.6 %while.39 = (s32[]{:T(128)}, f32[2,128,128]{2,1,0:T(8,128)S(1)}, s32[]{:T(128)}, bf16[16,2]{1,0:T(8,128)(2,1)S(1)}, bf16[16,2,128,128]{3,2,1,0:T(8,128)(2,1)}, /*index=5*/s32[]{:T(128)}, s32[]{:T(128)}) while((s32[]{:T(128)}, f32[2,128,128]{2,1,0:T(8,128)S(1)}, s32[]{:T(128)}, bf16[16,2]{1,0:T(8,128)(2,1)S(1)}, ...), condition=%wide.region_3.4_spmd.clone, body=%wide.region_2.3_spmd.clone.sunk | while | flops 163846 | bytes 327813 | solution.py:32
  82.7 2.1 convolution_convert_fusion.1
  84.8 44.3 %all-gather.6.cloned.1.call-done = bf16[4096,256]{1,0:T(8,128)(2,1)} async-done(((bf16[256,256]{1,0:T(8,128)(2,1)}), bf16[4096,256]{1,0:T(8,128)(2,1)}) %all-gather.6.cloned.1.call-update) | async-done | bytes 2097168 | tf_op jit(solution)/shard_map/all_gather | solution.py:133
  129.2 4.0 %reshape.143 = bf16[32,128,2,128]{3,2,1,0:T(2,128)(2,1)} reshape(bf16[4096,256]{1,0:T(8,128)(2,1)} %all-gather.6.cloned.1.call-done) | data formatting | bytes 4194304 | tf_op jit(solution)/shard_map/reshape | solution.py:137
  133.2 58.2 %all-gather.8.cloned.1.call-done = bf16[4096,256]{1,0:T(8,128)(2,1)} async-done(((bf16[256,256]{1,0:T(8,128)(2,1)}), bf16[4096,256]{1,0:T(8,128)(2,1)}) %all-gather.8.cloned.1.call-update) | async-done | bytes 2097168 | tf_op jit(solution)/shard_map/all_gather | solution.py:134
  191.4 4.0 %reshape.144 = bf16[32,128,2,128]{3,2,1,0:T(2,128)(2,1)} reshape(bf16[4096,256]{1,0:T(8,128)(2,1)} %all-gather.8.cloned.1.call-done) | data formatting | bytes 4194304 | tf_op jit(solution)/shard_map/reshape | solution.py:138
  195.4 165.2 %while.38 = (s32[]{:T(128)}, f32[2,128]{1,0:T(2,128)S(1)}, f32[2,128]{1,0:T(2,128)S(1)}, f32[128,2,128]{2,0,1:T(8,128)S(1)}, f32[2,128]{1,0:T(2,128)S(1)}, /*ind...) while((s32[]{:T(128)}, f32[2,128]{1,0:T(2,128)S(1)}, ...), condition=%wide.region_23.24_spmd.clone.clone, body=%wide.region_6.23_spmd.clone.clone.sunk | while | flops 34162200 | bytes 2311003 | solution.py:151
  198.6 1.0 constant_dynamic-slice_fusion.3
  204.0 1.0 constant_dynamic-slice_fusion.3
  209.4 1.0 constant_dynamic-slice_fusion.3
  214.7 1.0 constant_dynamic-slice_fusion.3
  220.1 1.0 constant_dynamic-slice_fusion.3
  225.5 1.0 constant_dynamic-slice_fusion.3
  230.8 1.0 constant_dynamic-slice_fusion.3
  236.2 1.0 constant_dynamic-slice_fusion.3
  241.6 1.0 constant_dynamic-slice_fusion.3
  360.9 3.6 convolution_convert_fusion
  364.6 17.0 %reduce-scatter.5.cloned.1.call-done = bf16[256,2048]{1,0:T(8,128)(2,1)} async-done(((bf16[256,4096]{1,0:T(8,128)(2,1)}), bf16[256,2048]{1,0:T(8,128)(2,1)}) %reduce-scatter.5.cloned.1.call-update) | async-done | bytes 1048592 | tf_op jit(solution)/shard_map/reduce_scatter | solution.py:174
  (617 shorter events, 119.2 us)
Async XLA Ops:
  7.2 75.5 %copy-start = (bf16[256,4096]{1,0:T(8,128)(2,1)S(1)}, bf16[256,4096]{1,0:T(8,128)(2,1)}, u32[]{:S(2)}) copy-start(bf16[256,4096]{1,0:T(8,128)(2,1)} %param.28) | copy-start | bytes 6291460
  7.2 59.0 %all-gather.10.cloned.1.call-start = ((), (), s32[]{:S(2)}) async-start(), calls=%async_computation.6 | async-start | bytes 1114112 | tf_op jit(solution)/shard_map/all_gather | solution.py:15
  10.3 71.5 %copy-start.2 = (bf16[256,256]{1,0:T(8,128)(2,1)S(1)}, bf16[256,256]{1,0:T(8,128)(2,1)}, u32[]{:S(2)}) copy-start(bf16[256,256]{1,0:T(8,128)(2,1)} %param.21) | copy-start | bytes 393220
  12.2 117.0 %all-gather.6.cloned.1.call-start = ((), (), s32[]{:S(2)}) async-start(), calls=%async_computation.3 | async-start | bytes 2228224 | tf_op jit(solution)/shard_map/all_gather | solution.py:133
  13.0 69.2 %copy-start.1 = (bf16[256,256]{1,0:T(8,128)(2,1)S(1)}, bf16[256,256]{1,0:T(8,128)(2,1)}, u32[]{:S(2)}) copy-start(bf16[256,256]{1,0:T(8,128)(2,1)} %param.23) | copy-start | bytes 393220
  13.0 178.4 %all-gather.8.cloned.1.call-start = ((), (), s32[]{:S(2)}) async-start(), calls=%async_computation.4 | async-start | bytes 2228224 | tf_op jit(solution)/shard_map/all_gather | solution.py:134
  13.7 350.8 %reduce-scatter.3.cloned.1.call-start = ((), (), s32[]{:S(2)}) async-start(), calls=%async_computation.2 | async-start | bytes 3145728 | tf_op jit(solution)/shard_map/reduce_scatter | solution.py:168
  84.8 296.8 %reduce-scatter.5.cloned.1.call-start = ((), (), s32[]{:S(2)}) async-start(), calls=%async_computation.5 | async-start | bytes 3145728 | tf_op jit(solution)/shard_map/reduce_scatter | solution.py:174
Sparse Core Ops, SparseCore 0:
  12.3 53.8 all-gather.9
  69.0 60.1 all-gather.5
  132.0 59.3 all-gather.7
  194.0 10.8 reduce-scatter.2
  364.6 16.8 reduce-scatter.4
where the time goes:
time: 393 us; the launch traced here: 388 us
  waiting for transfers between devices  142 us (36%)
  loops' own time  88.9 us (23%)
  local copies, waits for them, and re-layouts  63.6 us (16%)
  matrix products  31.5 us (8%)
  blocking collectives  27 us (7%)
  other arithmetic  20.2 us (5%)
  between operations  14.6 us (4%)
    another operation x1, loops' own time, softmax_heads(): carry, _ = lax.scan(inner, carry, (key_blocks, value_blocks, firsts))  85.6 us
    all_gather x1, waiting for transfers between devices, softmax_heads(): value_piece = lax.all_gather(v_soft, 'seq', axis=0, tiled=True)  58.2 us
    dynamic_slice x128, local copies, waits for them, and re-layouts, softmax_heads(): carry, _ = lax.scan(inner, carry, (key_blocks, value_blocks, firsts))  50.6 us
    all_gather x1, waiting for transfers between devices, softmax_heads(): key_piece = lax.all_gather(k_soft, 'seq', axis=0, tiled=True)  44.3 us
    unnamed x1, blocking collectives  27 us
    all_gather x1, waiting for transfers between devices, prefix(): lax.all_gather(part.astype(kind), axis)  21.1 us
    reduce_scatter x1, waiting for transfers between devices, local(): lax.psum_scatter(soft_term.astype(jnp.bfloat16).astype(jnp.float32).astyp...  17 us
    select_n x16, other arithmetic, turn(): return jax.tree.map(lambda a, b: jnp.where(reached, a, b), new, before)  14.9 us
  transfers between devices with their start and end apart: 5, of which 4 were waited for; matrix products, arithmetic and copies ran while one was open for 28% of the time, Pallas kernels for 0%

commit v1 on v0

v1 whole, which is shorter than its diff:
```python
import functools
import math

import jax
import jax.numpy as jnp
from jax import lax
from jax.experimental import pallas as pl
from jax.experimental.pallas import tpu as pltpu
from jax.sharding import PartitionSpec as P

HIGHEST = lax.Precision.HIGHEST
MESH = pl.DeviceIdType.MESH
F32 = jnp.float32
BF16 = jnp.bfloat16
PLANE = 4
NEG_BIG = -1e30


def dot(a, b, ca=1, cb=0, precision=None):
    return lax.dot_general(
        a, b, (((ca,), (cb,)), ((), ())), precision=precision, preferred_element_type=F32
    )


def split_dot(a, b):
    high = a.astype(BF16)
    low = (a - high.astype(F32)).astype(BF16)
    return dot(high, b) + dot(low, b)


def kernel(
    planes, groups, heads, factor,
    q_lin, k_lin, v_lin, decay, q_soft, k_soft, v_soft, wo_lin, wo_soft,
    lin_hbm, soft_hbm,
    q_in, k_in, v_in, vt, scores,
    s_own, s_in, d_own, d_in, t_own, t_in, e_own, e_in, carried, inside,
    o_out, o_in, l_out, l_in, o_self, l_self,
    gathered, weights, staged,
    q_ss, q_rs, k_ss, k_rs, v_ss, v_rs, s_ss, s_rs, d_ss, d_rs,
    t_ss, t_rs, e_ss, e_rs, o_ss, o_rs, l_ss, l_rs, w_ss, w_rs, g_ss, g_rs, w_ls, out_ls,
):
    rows = q_soft.shape[0]
    width = q_soft.shape[1] // heads
    columns = weights.shape[3]
    seq = lax.axis_index("seq")
    group = lax.axis_index("head")
    z, p = seq // PLANE, seq % PLANE
    x, y = p % 2, p // 2
    places = (p, 2 * y + 1 - x, 2 * (1 - y) + x, 3 - p)
    chips = tuple(z * PLANE + place for place in places)

    def remote(src, dst, ss, rs, **device):
        return pltpu.make_async_remote_copy(
            src_ref=src, dst_ref=dst, send_sem=ss, recv_sem=rs,
            device_id=device, device_id_type=MESH,
        )

    def cols(h):
        return slice(h * width, (h + 1) * width)

    barrier = pltpu.get_barrier_semaphore()
    for r in range(1, PLANE):
        pl.semaphore_signal(barrier, inc=1, device_id={"seq": chips[r]}, device_id_type=MESH)
    for k in range(1, planes):
        other = lax.rem(z + k, planes) * PLANE + p
        pl.semaphore_signal(barrier, inc=1, device_id={"seq": other}, device_id_type=MESH)
    for j in range(1, groups):
        peer = lax.rem(group + j, groups)
        pl.semaphore_signal(barrier, inc=1, device_id={"head": peer}, device_id_type=MESH)
    own_weights = []
    for layer, wo in enumerate((wo_lin, wo_soft)):
        piece = wo.at[:, pl.ds(pl.multiple_of(group * columns, 128), columns)]
        own_weights.append(
            pltpu.make_async_copy(piece, weights.at[layer, group], w_ls.at[layer])
        )
    for copy in own_weights:
        copy.start()
    pl.semaphore_wait(barrier, PLANE - 1 + planes - 1 + groups - 1)

    k_send = [remote(k_soft, k_in.at[r - 1], k_ss.at[r - 1], k_rs.at[r - 1], seq=chips[r]) for r in (1, 2)]
    v_send = [remote(v_soft, v_in.at[r - 1], v_ss.at[r - 1], v_rs.at[r - 1], seq=chips[r]) for r in (1, 2)]
    k_send[0].start()
    v_send[1].start()
    v_send[0].start()
    k_send[1].start()

    def query_copy(k):
        return remote(
            q_soft, q_in.at[k - 1], q_ss.at[k - 1], q_rs.at[k - 1], seq=(z - k) * PLANE + p
        )

    for k in range(1, planes):
        @pl.when(z >= k)
        def _(k=k):
            query_copy(k).start()

    weight_send = []
    for layer, wo in enumerate((wo_lin, wo_soft)):
        for j in range(1, groups):
            peer = lax.rem(group + j, groups)
            piece = wo.at[:, pl.ds(pl.multiple_of(peer * columns, 128), columns)]
            weight_send.append(
                remote(piece, weights.at[layer, group], w_ss.at[layer, j], w_rs.at[layer, j], head=peer)
            )
    for copy in weight_send:
        copy.start()

    before = lax.broadcasted_iota(jnp.int32, (rows, rows), 1)
    after = lax.broadcasted_iota(jnp.int32, (rows, rows), 0)
    lower = before <= after
    triangle = lower.astype(F32)
    sum_row = dot(decay[...], triangle, 1, 1, HIGHEST)
    sum_col = dot(triangle, decay[...], 1, 1, HIGHEST)
    d_own[...] = jnp.zeros_like(d_own)
    for h in range(heads):
        row = sum_row[h : h + 1, :]
        total = row[:, rows - 1 : rows]
        d_own[h : h + 1, :] = jnp.broadcast_to(total, (1, width))
        faded = k_lin[:, cols(h)].astype(F32).T * jnp.exp(total - row)
        s_own[cols(h), :] = split_dot(faded, v_lin[:, cols(h)]).astype(BF16)
    s_send = [
        remote(s_own, s_in.at[r - 1], s_ss.at[r - 1], s_rs.at[r - 1], seq=chips[r])
        for r in range(1, PLANE)
    ]
    d_send = [
        remote(d_own, d_in.at[r - 1], d_ss.at[r - 1], d_rs.at[r - 1], seq=chips[r])
        for r in range(1, PLANE)
    ]
    for copy in s_send + d_send:
        copy.start()

    for h in range(heads):
        gap = jnp.where(lower, sum_col[:, h : h + 1] - sum_row[h : h + 1, :], NEG_BIG)
        near = dot(q_lin[:, cols(h)], k_lin[:, cols(h)], 1, 1) * jnp.exp(gap)
        inside[:, cols(h)] = split_dot(near, v_lin[:, cols(h)])
    vt[0] = v_soft[...].T

    for copy in s_send + d_send:
        copy.wait_recv()
    spans = [d_own[...]] + [d_in[r] for r in range(PLANE - 1)]
    e_own[...] = sum(spans)
    for h in range(heads):
        whole = jnp.zeros((width, width), F32)
        earlier = jnp.zeros((width, width), F32)
        for r in range(PLANE):
            state = (s_own if r == 0 else s_in.at[r - 1])[cols(h), :].astype(F32)
            to_end = jnp.zeros((1, width), F32)
            to_here = jnp.zeros((1, width), F32)
            for other in range(PLANE):
                span = spans[other][h : h + 1, :]
                later = places[other] > places[r]
                to_end = to_end + jnp.where(later, span, 0.0)
                to_here = to_here + jnp.where(later & (places[other] < p), span, 0.0)
            whole = whole + jnp.exp(to_end) * state
            earlier = earlier + jnp.where(places[r] < p, jnp.exp(to_here), 0.0) * state
        t_own[cols(h), :] = whole.astype(BF16)
        carried[cols(h), :] = earlier

    def total_copies(k):
        there = (z + k) * PLANE + p
        return (
            remote(t_own, t_in.at[k - 1], t_ss.at[k - 1], t_rs.at[k - 1], seq=there),
            remote(e_own, e_in.at[k - 1], e_ss.at[k - 1], e_rs.at[k - 1], seq=there),
        )

    for k in range(1, planes):
        @pl.when(z + k < planes)
        def _(k=k):
            for copy in total_copies(k):
                copy.start()

    k_send[0].wait_recv()
    k_pass = remote(k_in.at[0], k_in.at[2], k_ss.at[2], k_rs.at[2], seq=chips[2])
    k_pass.start()
    v_send[1].wait_recv()
    v_pass = remote(v_in.at[1], v_in.at[2], v_ss.at[2], v_rs.at[2], seq=chips[1])
    v_pass.start()
    vt[2] = v_in[1].T
    v_send[0].wait_recv()
    vt[1] = v_in[0].T
    k_send[1].wait_recv()
    v_pass.wait_recv()
    vt[3] = v_in[2].T
    k_pass.wait_recv()

    scale = factor * math.log2(math.e)

    def attend(query, h, masked):
        top = None
        for r in range(PLANE):
            keys = (k_soft if r == 0 else k_in.at[r - 1])[:, cols(h)]
            part = dot(keys, query, 1, 1)
            if masked:
                allowed = after + places[r] * rows <= before + p * rows
                part = jnp.where(allowed, part, NEG_BIG)
            scores[h, r] = part
            best = jnp.max(part, axis=0, keepdims=True)
            top = best if top is None else jnp.maximum(top, best)
        total = jnp.zeros_like(top)
        result = jnp.zeros((width, rows), F32)
        for r in range(PLANE):
            weight = jnp.exp2((scores[h, r] - top) * scale)
            total = total + jnp.sum(weight, axis=0, keepdims=True)
            result = result + dot(vt[r, cols(h), :], weight.astype(BF16))
        return result / total, top * scale + jnp.log2(total)

    def output_copies(k):
        there = (z + k) * PLANE + p
        return (
            remote(o_out.at[k - 1], o_in.at[k - 1], o_ss.at[k - 1], o_rs.at[k - 1], seq=there),
            remote(l_out.at[k - 1], l_in.at[k - 1], l_ss.at[k - 1], l_rs.at[k - 1], seq=there),
        )

    for k in range(1, planes):
        @pl.when(z + k < planes)
        def _(k=k):
            query_copy(k).wait_recv()
            l_out[k - 1] = jnp.zeros(l_out.shape[1:], F32)
            for h in range(heads):
                result, level = attend(q_in[k - 1, :, cols(h)], h, False)
                o_out[k - 1, cols(h), :] = result.astype(BF16)
                l_out[k - 1, h : h + 1, :] = level
            for copy in output_copies(k):
                copy.start()

    for h in range(heads):
        result, level = attend(q_soft[:, cols(h)], h, True)
        o_self[cols(h), :] = result
        l_self[h : h + 1, :] = level

    for k in range(planes - 1, 0, -1):
        @pl.when(z >= k)
        def _(k=k):
            for copy in total_copies(k):
                copy.wait_recv()
    ahead = [jnp.where(places[r] < p, spans[r], 0.0) for r in range(PLANE)]
    reach = sum(ahead)
    for k in range(1, planes):
        @pl.when(z >= k)
        def _(k=k):
            gone = reach
            for nearer in range(1, k):
                gone = gone + e_in[nearer - 1]
            for h in range(heads):
                carried[cols(h), :] += jnp.exp(gone[h : h + 1, :]) * t_in[k - 1, cols(h), :].astype(F32)
    for h in range(heads):
        state = carried[cols(h), :]
        high = state.astype(BF16)
        low = (state - high.astype(F32)).astype(BF16)
        query = q_lin[:, cols(h)]
        raw = inside[:, cols(h)] + (dot(query, high) + dot(query, low)) * jnp.exp(sum_col[:, h : h + 1])
        norm = lax.rsqrt(jnp.mean(raw * raw, axis=-1, keepdims=True) + 1e-6)
        gathered[0, group, :, cols(h)] = (raw * norm).astype(BF16)

    def exchange(layer):
        return [
            remote(
                gathered.at[layer, group], gathered.at[layer, group],
                g_ss.at[layer, j], g_rs.at[layer, j], head=lax.rem(group + j, groups),
            )
            for j in range(1, groups)
        ]

    def project(layer, out_hbm):
        step = min(columns, 512)
        copies = []
        for c in range(columns // step):
            piece = pl.ds(c * step, step)
            total = jnp.zeros((rows, step), F32)
            for g in range(groups):
                total = total + dot(gathered[layer, g], weights[layer, g, :, piece])
            staged[layer, :, piece] = total.astype(BF16)
            copy = pltpu.make_async_copy(
                staged.at[layer, :, piece], out_hbm.at[:, piece], out_ls.at[layer, c]
            )
            copy.start()
            copies.append(copy)
        return copies

    lin_send = exchange(0)
    for copy in lin_send:
        copy.start()
    for copy in own_weights:
        copy.wait()
    for copy in weight_send:
        copy.wait_recv()
    for copy in lin_send:
        copy.wait_recv()
    out_copies = project(0, lin_hbm)

    for k in range(1, planes):
        @pl.when(z >= k)
        def _(k=k):
            for copy in output_copies(k):
                copy.wait_recv()
            for h in range(heads):
                mine, theirs = l_self[h : h + 1, :], l_in[k - 1, h : h + 1, :]
                level = jnp.maximum(mine, theirs)
                a, b = jnp.exp2(mine - level), jnp.exp2(theirs - level)
                both = a + b
                o_self[cols(h), :] = o_self[cols(h), :] * (a / both) + o_in[
                    k - 1, cols(h), :
                ].astype(F32) * (b / both)
                l_self[h : h + 1, :] = level + jnp.log2(both)
    gathered[1, group] = o_self[...].T.astype(BF16)
    soft_send = exchange(1)
    for copy in soft_send:
        copy.start()
    for copy in soft_send:
        copy.wait_recv()
    out_copies += project(1, soft_hbm)

    for copy in k_send + v_send + [k_pass, v_pass] + weight_send + s_send + d_send + lin_send + soft_send:
        copy.wait_send()
    for k in range(1, planes):
        @pl.when(z >= k)
        def _(k=k):
            query_copy(k).wait_send()

        @pl.when(z + k < planes)
        def _(k=k):
            for copy in total_copies(k) + output_copies(k):
                copy.wait_send()
    for copy in out_copies:
        copy.wait()


def local(planes, groups, *arrays):
    q_lin, _, _, decay, q_soft, _, _, wo_lin, _ = arrays
    rows, both = q_soft.shape
    heads = decay.shape[0]
    width = both // heads
    columns = wo_lin.shape[1] // groups
    far = max(planes - 1, 1)
    near = PLANE - 1
    vmem = pltpu.VMEM
    dma = pltpu.SemaphoreType.DMA
    scratch = [
        vmem((far, rows, both), BF16),
        vmem((near, rows, both), BF16),
        vmem((near, rows, both), BF16),
        vmem((PLANE, both, rows), BF16),
        vmem((heads, PLANE, rows, rows), F32),
        vmem((both, width), BF16),
        vmem((near, both, width), BF16),
        vmem((8, width), F32),
        vmem((near, 8, width), F32),
        vmem((both, width), BF16),
        vmem((far, both, width), BF16),
        vmem((8, width), F32),
        vmem((far, 8, width), F32),
        vmem((both, width), F32),
        vmem((rows, both), F32),
        vmem((far, both, rows), BF16),
        vmem((far, both, rows), BF16),
        vmem((far, 8, rows), F32),
        vmem((far, 8, rows), F32),
        vmem((both, rows), F32),
        vmem((8, rows), F32),
        vmem((2, groups, rows, both), BF16),
        vmem((2, groups, both, columns), BF16),
        vmem((2, rows, columns), BF16),
    ]
    pairs = [far, near, near, near, near, far, far, far, far]
    for count in pairs:
        scratch += [dma((count,)), dma((count,))]
    for _ in range(2):
        scratch += [dma((2, groups)), dma((2, groups))]
    scratch += [dma((2,)), dma((2, max(columns // min(columns, 512), 1)))]
    in_vmem = pl.BlockSpec(memory_space=pltpu.VMEM)
    anywhere = pl.BlockSpec(memory_space=pl.ANY)
    out = jax.ShapeDtypeStruct((rows, columns), BF16)
    return pl.pallas_call(
        functools.partial(kernel, planes, groups, heads, 1.0 / math.sqrt(width)),
        out_shape=(out, out),
        in_specs=[in_vmem] * 7 + [anywhere] * 2,
        out_specs=(anywhere, anywhere),
        scratch_shapes=scratch,
        compiler_params=pltpu.CompilerParams(
            collective_id=0, has_side_effects=True, vmem_limit_bytes=48 * 1024 * 1024
        ),
        name="attention_layers",
    )(*arrays)


def solution(mesh):
    planes = mesh.shape["seq"] // PLANE
    groups = mesh.shape["head"]
    in_specs = (P("seq", "head"),) * 3 + (P("head", "seq"),) + (P("seq", "head"),) * 3 + (P("head", None),) * 2
    out_specs = (P("seq", "head"), P("seq", "head"))
    return jax.shard_map(
        functools.partial(local, planes, groups),
        mesh=mesh, in_specs=in_specs, out_specs=out_specs, check_vma=False,
    )
```

time: 393 us -> 46.7 us (0.12); the launches traced: 388 us -> 46.4 us
  waiting for transfers between devices: 142 us -> 0 us
  loops' own time: 88.9 us -> 0 us
  local copies, waits for them, and re-layouts: 63.6 us -> 9.63 us
  Pallas kernels: 0 us -> 36.1 us
  matrix products: 31.5 us -> 0 us
  blocking collectives: 27 us -> 0 us
  other arithmetic: 20.2 us -> 0 us
  between operations: 14.6 us -> 0.66 us
    all_gather x3 -> x0, waiting for transfers between devices: 124 us -> none  [the longest x1 58.2 us: softmax_heads(): value_piece = lax.all_gather(v_soft, 'seq', axis=0, tiled=True)]
    another operation x81 -> x0, loops' own time: 88.9 us -> none  [the longest x1 85.6 us: softmax_heads(): carry, _ = lax.scan(inner, carry, (key_blocks, value_blocks, firsts))]
    dynamic_slice x128 -> x0, local copies, waits for them, and re-layouts: 50.6 us -> none  [softmax_heads(): carry, _ = lax.scan(inner, carry, (key_blocks, value_blocks, firsts))]
    pallas_call x0 -> x1, Pallas kernels: none -> 36.1 us  [local(): pl.pallas_call(functools.partial(kernel, planes, groups, heads, 1.0 / mat...]
    dot_general x108 -> x0, matrix products: 31.5 us -> none  [the longest x51 12.5 us: absorb(): jnp.einsum('hqk,khd->qhd', weights.astype(jnp.bfloat16), value_block, pre...]
    unnamed x1 -> x0, blocking collectives: 27 us -> none
    reduce_scatter x2 -> x0, waiting for transfers between devices: 17 us -> none  [the longest x1 17 us: local(): lax.psum_scatter(soft_term.astype(jnp.bfloat16).astype(jnp.float32).astyp...]
    select_n x16 -> x0, other arithmetic: 14.9 us -> none  [turn(): return jax.tree.map(lambda a, b: jnp.where(reached, a, b), new, before)]
  transfers between devices with their start and end apart: 5 -> 0, of which waited for: 4 -> 0; matrix products, arithmetic and copies ran while one was open for 28% -> 0% of each run, Pallas kernels for 0% -> 0%
where the time goes in v1:
time: 46.7 us; the launch traced here: 46.4 us
  Pallas kernels  36.1 us (77%)
  local copies, waits for them, and re-layouts  9.63 us (21%)
  between operations  0.66 us (1%)
    pallas_call x1, Pallas kernels, local(): pl.pallas_call(functools.partial(kernel, planes, groups, heads, 1.0 / mat...  36.1 us
    unnamed x18, local copies, waits for them, and re-layouts  9.63 us

profile of v1, /device:TPU:25, one launch (start us, length us, event | category | flops | bytes accessed | tf_op | source)
XLA Modules:
  0.0 46.4 jit_solution(7877202031239667699)
XLA Ops:
  0.6 0.0 copy-start
  0.6 1.6 %copy-done = bf16[256,4096]{1,0:T(8,128)(2,1)S(1)} copy-done((bf16[256,4096]{1,0:T(8,128)(2,1)S(1)}, bf16[256,4096]{1,0:T(8,128)(2,1)}, u32[]{:S(2)}) %copy-start) | copy-done | bytes 2097176
  2.2 0.0 copy-start.1
  2.2 0.9 %copy-done.1 = bf16[256,256]{1,0:T(8,128)(2,1)S(1)} copy-done((bf16[256,256]{1,0:T(8,128)(2,1)S(1)}, bf16[256,256]{1,0:T(8,128)(2,1)}, u32[]{:S(2)}) %copy-start.1) | copy-done | bytes 131096
  3.1 0.0 copy-start.2
  3.1 0.9 %copy-done.2 = bf16[256,256]{1,0:T(8,128)(2,1)S(1)} copy-done((bf16[256,256]{1,0:T(8,128)(2,1)S(1)}, bf16[256,256]{1,0:T(8,128)(2,1)}, u32[]{:S(2)}) %copy-start.2) | copy-done | bytes 131096
  4.0 0.0 copy-start.3
  4.0 0.9 %copy-done.3 = bf16[256,256]{1,0:T(8,128)(2,1)S(1)} copy-done((bf16[256,256]{1,0:T(8,128)(2,1)S(1)}, bf16[256,256]{1,0:T(8,128)(2,1)}, u32[]{:S(2)}) %copy-start.3) | copy-done | bytes 131096
  4.9 0.0 copy-start.4
  4.9 0.9 %copy-done.4 = bf16[256,256]{1,0:T(8,128)(2,1)S(1)} copy-done((bf16[256,256]{1,0:T(8,128)(2,1)S(1)}, bf16[256,256]{1,0:T(8,128)(2,1)}, u32[]{:S(2)}) %copy-start.4) | copy-done | bytes 131096
  5.8 0.0 copy-start.5
  5.8 0.9 %copy-done.5 = bf16[256,256]{1,0:T(8,128)(2,1)S(1)} copy-done((bf16[256,256]{1,0:T(8,128)(2,1)S(1)}, bf16[256,256]{1,0:T(8,128)(2,1)}, u32[]{:S(2)}) %copy-start.5) | copy-done | bytes 131096
  6.7 0.0 copy-start.6
  6.8 0.9 %copy-done.6 = bf16[256,256]{1,0:T(8,128)(2,1)S(1)} copy-done((bf16[256,256]{1,0:T(8,128)(2,1)S(1)}, bf16[256,256]{1,0:T(8,128)(2,1)}, u32[]{:S(2)}) %copy-start.6) | copy-done | bytes 131096
  7.7 0.0 copy-start.7
  7.7 0.7 %copy-done.7 = f32[2,256]{1,0:T(2,128)S(1)} copy-done((f32[2,256]{1,0:T(2,128)S(1)}, f32[2,256]{1,0:T(2,128)}, u32[]{:S(2)}) %copy-start.7) | copy-done | bytes 2072
  8.3 36.1 %attention_layers.1 = (bf16[256,2048]{1,0:T(8,128)(2,1)S(1)}, bf16[256,2048]{1,0:T(8,128)(2,1)S(1)}) custom-call(bf16[256,256]{1,0:T(8,128)(2,1)S(1)} %copy-done.1, bf16[256,256]{1,0:T(8,128)(2,1)S(1)} %copy-done.2, bf16[256,256]{1,0:T(8,128)(2,1)S(1)} %copy-done.3, f32[2,256]{1,0:T(2,128)S(1)} %copy-done.7, bf16[256,256]{1,0:T(8,128)(2,1)S(1)} %copy-done.4, ...), custom_call_target="tpu_custom_call" | custom-call | tf_op jit(solution)/shard_map/attention_layers/pallas_call | solution.py:373
  44.5 1.0 %copy.13 = bf16[256,2048]{1,0:T(8,128)(2,1)} copy(bf16[256,2048]{1,0:T(8,128)(2,1)S(1)} %get-tuple-element.4) | data formatting | bytes 2097152
  45.4 1.0 %copy.14 = bf16[256,2048]{1,0:T(8,128)(2,1)} copy(bf16[256,2048]{1,0:T(8,128)(2,1)S(1)} %get-tuple-element.5) | data formatting | bytes 2097152
Async XLA Ops:
  0.6 1.6 %copy-start = (bf16[256,4096]{1,0:T(8,128)(2,1)S(1)}, bf16[256,4096]{1,0:T(8,128)(2,1)}, u32[]{:S(2)}) copy-start(bf16[256,4096]{1,0:T(8,128)(2,1)} %wo_lin.1) | copy-start | bytes 6291460
  2.2 0.9 %copy-start.1 = (bf16[256,256]{1,0:T(8,128)(2,1)S(1)}, bf16[256,256]{1,0:T(8,128)(2,1)}, u32[]{:S(2)}) copy-start(bf16[256,256]{1,0:T(8,128)(2,1)} %q_lin.1) | copy-start | bytes 393220
  3.1 0.9 %copy-start.2 = (bf16[256,256]{1,0:T(8,128)(2,1)S(1)}, bf16[256,256]{1,0:T(8,128)(2,1)}, u32[]{:S(2)}) copy-start(bf16[256,256]{1,0:T(8,128)(2,1)} %k_lin.1) | copy-start | bytes 393220
  4.0 0.9 %copy-start.3 = (bf16[256,256]{1,0:T(8,128)(2,1)S(1)}, bf16[256,256]{1,0:T(8,128)(2,1)}, u32[]{:S(2)}) copy-start(bf16[256,256]{1,0:T(8,128)(2,1)} %v_lin.1) | copy-start | bytes 393220
  4.9 0.9 %copy-start.4 = (bf16[256,256]{1,0:T(8,128)(2,1)S(1)}, bf16[256,256]{1,0:T(8,128)(2,1)}, u32[]{:S(2)}) copy-start(bf16[256,256]{1,0:T(8,128)(2,1)} %q_soft.1) | copy-start | bytes 393220
  5.8 0.9 %copy-start.5 = (bf16[256,256]{1,0:T(8,128)(2,1)S(1)}, bf16[256,256]{1,0:T(8,128)(2,1)}, u32[]{:S(2)}) copy-start(bf16[256,256]{1,0:T(8,128)(2,1)} %k_soft.1) | copy-start | bytes 393220
  6.7 0.9 %copy-start.6 = (bf16[256,256]{1,0:T(8,128)(2,1)S(1)}, bf16[256,256]{1,0:T(8,128)(2,1)}, u32[]{:S(2)}) copy-start(bf16[256,256]{1,0:T(8,128)(2,1)} %v_soft.1) | copy-start | bytes 393220
  7.7 0.7 %copy-start.7 = (f32[2,256]{1,0:T(2,128)S(1)}, f32[2,256]{1,0:T(2,128)}, u32[]{:S(2)}) copy-start(f32[2,256]{1,0:T(2,128)} %decay.1) | copy-start | bytes 6148

commit v2 on v1

--- a/solution.py
+++ b/solution.py
@@ -30,14 +30,15 @@
 
 def kernel(
     planes, groups, heads, factor,
-    q_lin, k_lin, v_lin, decay, q_soft, k_soft, v_soft, wo_lin, wo_soft,
+    q_lin_hbm, k_lin_hbm, v_lin_hbm, decay_hbm, q_hbm, k_hbm, v_hbm, wo_lin, wo_soft,
     lin_hbm, soft_hbm,
+    q_lin, k_lin, v_lin, decay, q_soft, k_soft, v_soft, totals,
     q_in, k_in, v_in, vt, scores,
     s_own, s_in, d_own, d_in, t_own, t_in, e_own, e_in, carried, inside,
     o_out, o_in, l_out, l_in, o_self, l_self,
     gathered, weights, staged,
     q_ss, q_rs, k_ss, k_rs, v_ss, v_rs, s_ss, s_rs, d_ss, d_rs,
-    t_ss, t_rs, e_ss, e_rs, o_ss, o_rs, l_ss, l_rs, w_ss, w_rs, g_ss, g_rs, w_ls, out_ls,
+    t_ss, t_rs, e_ss, e_rs, o_ss, o_rs, l_ss, l_rs, w_ss, w_rs, g_ss, g_rs, w_ls, out_ls, in_ls,
 ):
     rows = q_soft.shape[0]
     width = q_soft.shape[1] // heads
@@ -57,6 +58,16 @@
 
     def cols(h):
         return slice(h * width, (h + 1) * width)
+
+    loads = [
+        pltpu.make_async_copy(src, dst, in_ls.at[i])
+        for i, (src, dst) in enumerate((
+            (decay_hbm, decay), (k_lin_hbm, k_lin), (v_lin_hbm, v_lin), (q_lin_hbm, q_lin),
+            (v_hbm, v_soft), (k_hbm, k_soft), (q_hbm, q_soft),
+        ))
+    ]
+    for copy in loads:
+        copy.start()
 
     barrier = pltpu.get_barrier_semaphore()
     for r in range(1, PLANE):
@@ -77,8 +88,8 @@
         copy.start()
     pl.semaphore_wait(barrier, PLANE - 1 + planes - 1 + groups - 1)
 
-    k_send = [remote(k_soft, k_in.at[r - 1], k_ss.at[r - 1], k_rs.at[r - 1], seq=chips[r]) for r in (1, 2)]
-    v_send = [remote(v_soft, v_in.at[r - 1], v_ss.at[r - 1], v_rs.at[r - 1], seq=chips[r]) for r in (1, 2)]
+    k_send = [remote(k_hbm, k_in.at[r - 1], k_ss.at[r - 1], k_rs.at[r - 1], seq=chips[r]) for r in (1, 2)]
+    v_send = [remote(v_hbm, v_in.at[r - 1], v_ss.at[r - 1], v_rs.at[r - 1], seq=chips[r]) for r in (1, 2)]
     k_send[0].start()
     v_send[1].start()
     v_send[0].start()
@@ -86,10 +97,10 @@
 
     def query_copy(k):
         return remote(
-            q_soft, q_in.at[k - 1], q_ss.at[k - 1], q_rs.at[k - 1], seq=(z - k) * PLANE + p
+            q_hbm, q_in.at[k - 1], q_ss.at[k - 1], q_rs.at[k - 1], seq=(z - k) * PLANE + p
         )
 
-    for k in range(1, planes):
+    for k in range(planes - 1, 0, -1):
         @pl.when(z >= k)
         def _(k=k):
             query_copy(k).start()
@@ -108,6 +119,8 @@
     before = lax.broadcasted_iota(jnp.int32, (rows, rows), 1)
     after = lax.broadcasted_iota(jnp.int32, (rows, rows), 0)
     lower = before <= after
+    for copy in loads[:3]:
+        copy.wait()
     triangle = lower.astype(F32)
     sum_row = dot(decay[...], triangle, 1, 1, HIGHEST)
     sum_col = dot(triangle, decay[...], 1, 1, HIGHEST)
@@ -129,6 +142,8 @@
     for copy in s_send + d_send:
         copy.start()
 
+    for copy in loads[3:]:
+        copy.wait()
     for h in range(heads):
         gap = jnp.where(lower, sum_col[:, h : h + 1] - sum_row[h : h + 1, :], NEG_BIG)
         near = dot(q_lin[:, cols(h)], k_lin[:, cols(h)], 1, 1) * jnp.exp(gap)
@@ -175,58 +190,93 @@
     v_send[1].wait_recv()
     v_pass = remote(v_in.at[1], v_in.at[2], v_ss.at[2], v_rs.at[2], seq=chips[1])
     v_pass.start()
+
+    scale = factor * math.log2(math.e)
+
+    def score(query, h, r, top=None, masked=False):
+        keys = (k_soft if r == 0 else k_in.at[r - 1])[:, cols(h)]
+        part = dot(keys, query, 1, 1)
+        if masked:
+            part = jnp.where(after <= before, part, NEG_BIG)
+        scores[h, r] = part
+        best = jnp.max(part, axis=0, keepdims=True)
+        return best if top is None else jnp.maximum(top, best)
+
+    def finish(h, slots, top):
+        total = jnp.zeros_like(top)
+        result = jnp.zeros((width, rows), F32)
+        for r in slots:
+            weight = jnp.exp2((scores[h, r] - top) * scale)
+            total = total + jnp.sum(weight, axis=0, keepdims=True)
+            result = result + dot(vt[r, cols(h), :], weight.astype(BF16))
+        return result / total, top * scale + jnp.log2(total)
+
+    def merge(h, theirs, level_there):
+        mine = l_self[h : h + 1, :]
+        level = jnp.maximum(mine, level_there)
+        a, b = jnp.exp2(mine - level), jnp.exp2(level_there - level)
+        both = a + b
+        o_self[cols(h), :] = o_self[cols(h), :] * (a / both) + theirs * (b / both)
+        l_self[h : h + 1, :] = level + jnp.log2(both)
+
+    for h in range(heads):
+        top = score(q_soft[:, cols(h)], h, 0, masked=True)
+        o_self[cols(h), :], l_self[h : h + 1, :] = finish(h, (0,), top)
     vt[2] = v_in[1].T
     v_send[0].wait_recv()
     vt[1] = v_in[0].T
     k_send[1].wait_recv()
-    v_pass.wait_recv()
-    vt[3] = v_in[2].T
-    k_pass.wait_recv()
-
-    scale = factor * math.log2(math.e)
-
-    def attend(query, h, masked):
-        top = None
-        for r in range(PLANE):
-            keys = (k_soft if r == 0 else k_in.at[r - 1])[:, cols(h)]
-            part = dot(keys, query, 1, 1)
-            if masked:
-                allowed = after + places[r] * rows <= before + p * rows
-                part = jnp.where(allowed, part, NEG_BIG)
-            scores[h, r] = part
-            best = jnp.max(part, axis=0, keepdims=True)
-            top = best if top is None else jnp.maximum(top, best)
-        total = jnp.zeros_like(top)
-        result = jnp.zeros((width, rows), F32)
-        for r in range(PLANE):
-            weight = jnp.exp2((scores[h, r] - top) * scale)
-            total = total + jnp.sum(weight, axis=0, keepdims=True)
-            result = result + dot(vt[r, cols(h), :], weight.astype(BF16))
-        return result / total, top * scale + jnp.log2(total)
+
+    def last_slot():
+        k_pass.wait_recv()
+        v_pass.wait_recv()
+        vt[3] = v_in[2].T
 
     def output_copies(k):
         there = (z + k) * PLANE + p
-        return (
-            remote(o_out.at[k - 1], o_in.at[k - 1], o_ss.at[k - 1], o_rs.at[k - 1], seq=there),
-            remote(l_out.at[k - 1], l_in.at[k - 1], l_ss.at[k - 1], l_rs.at[k - 1], seq=there),
-        )
-
-    for k in range(1, planes):
-        @pl.when(z + k < planes)
-        def _(k=k):
+        copies = [
+            remote(
+                o_out.at[k - 1, cols(h)], o_in.at[k - 1, cols(h)],
+                o_ss.at[k - 1, h], o_rs.at[k - 1, h], seq=there,
+            )
+            for h in range(heads)
+        ]
+        return copies + [
+            remote(l_out.at[k - 1], l_in.at[k - 1], l_ss.at[k - 1], l_rs.at[k - 1], seq=there)
+        ]
+
+    for target in range(planes - 1, 0, -1):
+        @pl.when(z < target)
+        def _(target=target):
+            k = target - z
             query_copy(k).wait_recv()
+            copies = output_copies(k)
             l_out[k - 1] = jnp.zeros(l_out.shape[1:], F32)
+            queries = [q_in[k - 1, :, cols(h)] for h in range(heads)]
+            tops = [None] * heads
             for h in range(heads):
-                result, level = attend(q_in[k - 1, :, cols(h)], h, False)
+                for r in range(PLANE - 1):
+                    tops[h] = score(queries[h], h, r, tops[h])
+            if target == planes - 1:
+                last_slot()
+            for h in range(heads):
+                tops[h] = score(queries[h], h, PLANE - 1, tops[h])
+                result, level = finish(h, range(PLANE), tops[h])
                 o_out[k - 1, cols(h), :] = result.astype(BF16)
                 l_out[k - 1, h : h + 1, :] = level
-            for copy in output_copies(k):
-                copy.start()
-
-    for h in range(heads):
-        result, level = attend(q_soft[:, cols(h)], h, True)
-        o_self[cols(h), :] = result
-        l_self[h : h + 1, :] = level
+                copies[h].start()
+            copies[heads].start()
+
+    @pl.when(z == planes - 1)
+    def _():
+        last_slot()
+
+    for r in range(1, PLANE):
+        @pl.when(places[r] < p)
+        def _(r=r):
+            for h in range(heads):
+                top = score(q_soft[:, cols(h)], h, r)
+                merge(h, *finish(h, (r,), top))
 
     for k in range(planes - 1, 0, -1):
         @pl.when(z >= k)
@@ -261,13 +311,20 @@
             for j in range(1, groups)
         ]
 
-    def project(layer, out_hbm):
-        step = min(columns, 512)
+    step = min(columns, 512)
+
+    def project_own(layer):
+        for c in range(columns // step):
+            piece = pl.ds(c * step, step)
+            totals[:, piece] = dot(gathered[layer, group], weights[layer, group, :, piece])
+
+    def project_others(layer, out_hbm):
         copies = []
         for c in range(columns // step):
             piece = pl.ds(c * step, step)
-            total = jnp.zeros((rows, step), F32)
-            for g in range(groups):
+            total = totals[:, piece]
+            for j in range(1, groups):
+                g = lax.rem(group + j, groups)
                 total = total + dot(gathered[layer, g], weights[layer, g, :, piece])
             staged[layer, :, piece] = total.astype(BF16)
             copy = pltpu.make_async_copy(
@@ -282,11 +339,12 @@
         copy.start()
     for copy in own_weights:
         copy.wait()
+    project_own(0)
     for copy in weight_send:
         copy.wait_recv()
     for copy in lin_send:
         copy.wait_recv()
-    out_copies = project(0, lin_hbm)
+    out_copies = project_others(0, lin_hbm)
 
     for k in range(1, planes):
         @pl.when(z >= k)
@@ -294,21 +352,15 @@
             for copy in output_copies(k):
                 copy.wait_recv()
             for h in range(heads):
-                mine, theirs = l_self[h : h + 1, :], l_in[k - 1, h : h + 1, :]
-                level = jnp.maximum(mine, theirs)
-                a, b = jnp.exp2(mine - level), jnp.exp2(theirs - level)
-                both = a + b
-                o_self[cols(h), :] = o_self[cols(h), :] * (a / both) + o_in[
-                    k - 1, cols(h), :
-                ].astype(F32) * (b / both)
-                l_self[h : h + 1, :] = level + jnp.log2(both)
+                merge(h, o_in[k - 1, cols(h), :].astype(F32), l_in[k - 1, h : h + 1, :])
     gathered[1, group] = o_self[...].T.astype(BF16)
     soft_send = exchange(1)
     for copy in soft_send:
         copy.start()
+    project_own(1)
     for copy in soft_send:
         copy.wait_recv()
-    out_copies += project(1, soft_hbm)
+    out_copies += project_others(1, soft_hbm)
 
     for copy in k_send + v_send + [k_pass, v_pass] + weight_send + s_send + d_send + lin_send + soft_send:
         copy.wait_send()
@@ -319,7 +371,7 @@
 
         @pl.when(z + k < planes)
         def _(k=k):
-            for copy in total_copies(k) + output_copies(k):
+            for copy in list(total_copies(k)) + output_copies(k):
                 copy.wait_send()
     for copy in out_copies:
         copy.wait()
@@ -336,6 +388,14 @@
     vmem = pltpu.VMEM
     dma = pltpu.SemaphoreType.DMA
     scratch = [
+        vmem((rows, both), BF16),
+        vmem((rows, both), BF16),
+        vmem((rows, both), BF16),
+        vmem(decay.shape, F32),
+        vmem((rows, both), BF16),
+        vmem((rows, both), BF16),
+        vmem((rows, both), BF16),
+        vmem((rows, columns), F32),
         vmem((far, rows, both), BF16),
         vmem((near, rows, both), BF16),
         vmem((near, rows, both), BF16),
@@ -361,23 +421,22 @@
         vmem((2, groups, both, columns), BF16),
         vmem((2, rows, columns), BF16),
     ]
-    pairs = [far, near, near, near, near, far, far, far, far]
-    for count in pairs:
-        scratch += [dma((count,)), dma((count,))]
+    pairs = [(far,)] + [(near,)] * 4 + [(far,)] * 2 + [(far, heads), (far,)]
+    for shape in pairs:
+        scratch += [dma(shape), dma(shape)]
     for _ in range(2):
         scratch += [dma((2, groups)), dma((2, groups))]
-    scratch += [dma((2,)), dma((2, max(columns // min(columns, 512), 1)))]
-    in_vmem = pl.BlockSpec(memory_space=pltpu.VMEM)
+    scratch += [dma((2,)), dma((2, columns // min(columns, 512))), dma((7,))]
     anywhere = pl.BlockSpec(memory_space=pl.ANY)
     out = jax.ShapeDtypeStruct((rows, columns), BF16)
     return pl.pallas_call(
         functools.partial(kernel, planes, groups, heads, 1.0 / math.sqrt(width)),
         out_shape=(out, out),
-        in_specs=[in_vmem] * 7 + [anywhere] * 2,
+        in_specs=[anywhere] * 9,
         out_specs=(anywhere, anywhere),
         scratch_shapes=scratch,
         compiler_params=pltpu.CompilerParams(
-            collective_id=0, has_side_effects=True, vmem_limit_bytes=48 * 1024 * 1024
+            collective_id=0, has_side_effects=True, vmem_limit_bytes=60 * 1024 * 1024
         ),
         name="attention_layers",
     )(*arrays)

time: 46.7 us -> 40.7 us (0.87)
  the two profiles are of different devices: /device:TPU:25 before, /device:TPU:17 now
where the time goes in v2:
time: 40.7 us; the launch traced here: 40.6 us
  Pallas kernels  36.5 us (90%)
  local copies, waits for them, and re-layouts  3.37 us (8%)
  between operations  0.65 us (2%)
    pallas_call x1, Pallas kernels, local(): pl.pallas_call(functools.partial(kernel, planes, groups, heads, 1.0 / mat...  36.5 us
    unnamed x4, local copies, waits for them, and re-layouts  3.37 us

profile of v2, /device:TPU:17, one launch (start us, length us, event | category | flops | bytes accessed | tf_op | source)
XLA Modules:
  0.0 40.6 jit_solution(9067884036027896596)
XLA Ops:
  0.6 36.5 %attention_layers.1 = (bf16[256,2048]{1,0:T(8,128)(2,1)}, bf16[256,2048]{1,0:T(8,128)(2,1)}) custom-call(bf16[256,256]{1,0:T(8,128)(2,1)} %q_lin_hbm.1, bf16[256,256]{1,0:T(8,128)(2,1)} %k_lin_hbm.1, bf16[256,256]{1,0:T(8,128)(2,1)} %v_lin_hbm.1, f32[2,256]{1,0:T(2,128)} %decay_hbm.1, bf16[256,256]{1,0:T(8,128)(2,1)} %q_hbm.1, bf16[256,256]{1,0:T(8,128)(2,1)} %k_hbm.1, ...), custom_call_target="tpu_custom_call" | custom-call | tf_op jit(solution)/shard_map/attention_layers/pallas_call | solution.py:432
  37.2 0.0 copy-start
  37.2 2.4 %copy.13 = bf16[256,2048]{1,0:T(8,128)(2,1)} copy(bf16[256,2048]{1,0:T(8,128)(2,1)} %get-tuple-element.4) | data formatting | bytes 2097152
  39.6 0.0 copy-done
  39.6 1.0 %copy.14 = bf16[256,2048]{1,0:T(8,128)(2,1)} copy(bf16[256,2048]{1,0:T(8,128)(2,1)S(1)} %copy-done) | data formatting | bytes 2097152
Async XLA Ops:
  37.2 2.4 %copy-start = (bf16[256,2048]{1,0:T(8,128)(2,1)S(1)}, bf16[256,2048]{1,0:T(8,128)(2,1)}, u32[]{:S(2)}) copy-start(bf16[256,2048]{1,0:T(8,128)(2,1)} %get-tuple-element.5) | copy-start | bytes 3145732

commit v3 on v2

--- a/solution.py
+++ b/solution.py
@@ -35,7 +35,7 @@
     q_lin, k_lin, v_lin, decay, q_soft, k_soft, v_soft, totals,
     q_in, k_in, v_in, vt, scores,
     s_own, s_in, d_own, d_in, t_own, t_in, e_own, e_in, carried, inside,
-    o_out, o_in, l_out, l_in, o_self, l_self,
+    o_part, o_out, o_in, l_out, l_in, o_self, l_self,
     gathered, weights, staged,
     q_ss, q_rs, k_ss, k_rs, v_ss, v_rs, s_ss, s_rs, d_ss, d_rs,
     t_ss, t_rs, e_ss, e_rs, o_ss, o_rs, l_ss, l_rs, w_ss, w_rs, g_ss, g_rs, w_ls, out_ls, in_ls,
@@ -211,13 +211,16 @@
             result = result + dot(vt[r, cols(h), :], weight.astype(BF16))
         return result / total, top * scale + jnp.log2(total)
 
+    def merged(mine, level_here, theirs, level_there):
+        level = jnp.maximum(level_here, level_there)
+        a, b = jnp.exp2(level_here - level), jnp.exp2(level_there - level)
+        both = a + b
+        return mine * (a / both) + theirs * (b / both), level + jnp.log2(both)
+
     def merge(h, theirs, level_there):
-        mine = l_self[h : h + 1, :]
-        level = jnp.maximum(mine, level_there)
-        a, b = jnp.exp2(mine - level), jnp.exp2(level_there - level)
-        both = a + b
-        o_self[cols(h), :] = o_self[cols(h), :] * (a / both) + theirs * (b / both)
-        l_self[h : h + 1, :] = level + jnp.log2(both)
+        o_self[cols(h), :], l_self[h : h + 1, :] = merged(
+            o_self[cols(h), :], l_self[h : h + 1, :], theirs, level_there
+        )
 
     for h in range(heads):
         top = score(q_soft[:, cols(h)], h, 0, masked=True)
@@ -232,26 +235,24 @@
         v_pass.wait_recv()
         vt[3] = v_in[2].T
 
-    def output_copies(k):
-        there = (z + k) * PLANE + p
-        copies = [
+    def output_copies(k, h):
+        there = (z + 1) * PLANE + p
+        return (
             remote(
                 o_out.at[k - 1, cols(h)], o_in.at[k - 1, cols(h)],
                 o_ss.at[k - 1, h], o_rs.at[k - 1, h], seq=there,
-            )
-            for h in range(heads)
-        ]
-        return copies + [
-            remote(l_out.at[k - 1], l_in.at[k - 1], l_ss.at[k - 1], l_rs.at[k - 1], seq=there)
-        ]
+            ),
+            remote(
+                l_out.at[k - 1, h], l_in.at[k - 1, h],
+                l_ss.at[k - 1, h], l_rs.at[k - 1, h], seq=there,
+            ),
+        )
 
     for target in range(planes - 1, 0, -1):
         @pl.when(z < target)
         def _(target=target):
             k = target - z
             query_copy(k).wait_recv()
-            copies = output_copies(k)
-            l_out[k - 1] = jnp.zeros(l_out.shape[1:], F32)
             queries = [q_in[k - 1, :, cols(h)] for h in range(heads)]
             tops = [None] * heads
             for h in range(heads):
@@ -262,21 +263,46 @@
             for h in range(heads):
                 tops[h] = score(queries[h], h, PLANE - 1, tops[h])
                 result, level = finish(h, range(PLANE), tops[h])
-                o_out[k - 1, cols(h), :] = result.astype(BF16)
-                l_out[k - 1, h : h + 1, :] = level
-                copies[h].start()
-            copies[heads].start()
+                o_part[k - 1, cols(h), :] = result
+                l_out[k - 1, h] = jnp.broadcast_to(level, (8, rows))
+
+                @pl.when(z == 0)
+                def _(h=h, k=k):
+                    o_out[k - 1, cols(h), :] = o_part[k - 1, cols(h), :].astype(BF16)
+                    for copy in output_copies(k, h):
+                        copy.start()
 
     @pl.when(z == planes - 1)
     def _():
         last_slot()
 
-    for r in range(1, PLANE):
-        @pl.when(places[r] < p)
-        def _(r=r):
+    def own_rows(chosen):
+        for r in range(1, PLANE):
+            @pl.when(chosen & (places[r] < p))
+            def _(r=r):
+                for h in range(heads):
+                    top = score(q_soft[:, cols(h)], h, r)
+                    merge(h, *finish(h, (r,), top))
+
+    own_rows(z >= 2)
+
+    for target in range(planes - 1, 1, -1):
+        @pl.when((z >= 1) & (z < target))
+        def _(target=target):
+            k = target - z
             for h in range(heads):
-                top = score(q_soft[:, cols(h)], h, r)
-                merge(h, *finish(h, (r,), top))
+                for copy in output_copies(k + 1, h):
+                    copy.wait_recv()
+                result, level = merged(
+                    o_part[k - 1, cols(h), :], l_out[k - 1, h, 0:1, :],
+                    o_in[k, cols(h), :].astype(F32), l_in[k, h, 0:1, :],
+                )
+                o_out[k - 1, cols(h), :] = result.astype(BF16)
+                l_out[k - 1, h] = jnp.broadcast_to(level, (8, rows))
+                for copy in output_copies(k, h):
+                    copy.start()
+
+    own_rows(z < 2)
 
     for k in range(planes - 1, 0, -1):
         @pl.when(z >= k)
@@ -346,13 +372,13 @@
         copy.wait_recv()
     out_copies = project_others(0, lin_hbm)
 
-    for k in range(1, planes):
-        @pl.when(z >= k)
-        def _(k=k):
-            for copy in output_copies(k):
+    @pl.when(z >= 1)
+    def _():
+        for h in range(heads):
+            for copy in output_copies(1, h):
                 copy.wait_recv()
-            for h in range(heads):
-                merge(h, o_in[k - 1, cols(h), :].astype(F32), l_in[k - 1, h : h + 1, :])
+            merge(h, o_in[0, cols(h), :].astype(F32), l_in[0, h, 0:1, :])
+
     gathered[1, group] = o_self[...].T.astype(BF16)
     soft_send = exchange(1)
     for copy in soft_send:
@@ -371,8 +397,11 @@
 
         @pl.when(z + k < planes)
         def _(k=k):
-            for copy in list(total_copies(k)) + output_copies(k):
+            for copy in total_copies(k):
                 copy.wait_send()
+            for h in range(heads):
+                for copy in output_copies(k, h):
+                    copy.wait_send()
     for copy in out_copies:
         copy.wait()
 
@@ -411,17 +440,18 @@
         vmem((far, 8, width), F32),
         vmem((both, width), F32),
         vmem((rows, both), F32),
+        vmem((far, both, rows), F32),
         vmem((far, both, rows), BF16),
         vmem((far, both, rows), BF16),
-        vmem((far, 8, rows), F32),
-        vmem((far, 8, rows), F32),
+        vmem((far, heads, 8, rows), F32),
+        vmem((far, heads, 8, rows), F32),
         vmem((both, rows), F32),
         vmem((8, rows), F32),
         vmem((2, groups, rows, both), BF16),
         vmem((2, groups, both, columns), BF16),
         vmem((2, rows, columns), BF16),
     ]
-    pairs = [(far,)] + [(near,)] * 4 + [(far,)] * 2 + [(far, heads), (far,)]
+    pairs = [(far,)] + [(near,)] * 4 + [(far,)] * 2 + [(far, heads)] * 2
     for shape in pairs:
         scratch += [dma(shape), dma(shape)]
     for _ in range(2):

time: 40.7 us -> 38.8 us (0.953)
  the two profiles are of different devices: /device:TPU:17 before, /device:TPU:25 now
where the time goes in v3:
time: 38.8 us; the launch traced here: 38.6 us
  Pallas kernels  34.6 us (89%)
  local copies, waits for them, and re-layouts  3.37 us (9%)
  between operations  0.65 us (2%)
    pallas_call x1, Pallas kernels, local(): pl.pallas_call(functools.partial(kernel, planes, groups, heads, 1.0 / mat...  34.6 us
    unnamed x4, local copies, waits for them, and re-layouts  3.37 us

profile of v3, /device:TPU:25, one launch (start us, length us, event | category | flops | bytes accessed | tf_op | source)
XLA Modules:
  0.0 38.6 jit_solution(5351162357121358159)
XLA Ops:
  0.6 34.6 %attention_layers.1 = (bf16[256,2048]{1,0:T(8,128)(2,1)}, bf16[256,2048]{1,0:T(8,128)(2,1)}) custom-call(bf16[256,256]{1,0:T(8,128)(2,1)} %q_lin_hbm.1, bf16[256,256]{1,0:T(8,128)(2,1)} %k_lin_hbm.1, bf16[256,256]{1,0:T(8,128)(2,1)} %v_lin_hbm.1, f32[2,256]{1,0:T(2,128)} %decay_hbm.1, bf16[256,256]{1,0:T(8,128)(2,1)} %q_hbm.1, bf16[256,256]{1,0:T(8,128)(2,1)} %k_hbm.1, ...), custom_call_target="tpu_custom_call" | custom-call | tf_op jit(solution)/shard_map/attention_layers/pallas_call | solution.py:462
  35.3 0.0 copy-start
  35.3 2.4 %copy.13 = bf16[256,2048]{1,0:T(8,128)(2,1)} copy(bf16[256,2048]{1,0:T(8,128)(2,1)} %get-tuple-element.4) | data formatting | bytes 2097152
  37.7 0.0 copy-done
  37.7 1.0 %copy.14 = bf16[256,2048]{1,0:T(8,128)(2,1)} copy(bf16[256,2048]{1,0:T(8,128)(2,1)S(1)} %copy-done) | data formatting | bytes 2097152
Async XLA Ops:
  35.3 2.4 %copy-start = (bf16[256,2048]{1,0:T(8,128)(2,1)S(1)}, bf16[256,2048]{1,0:T(8,128)(2,1)}, u32[]{:S(2)}) copy-start(bf16[256,2048]{1,0:T(8,128)(2,1)} %get-tuple-element.5) | copy-start | bytes 3145732

commit v4 on v3

--- a/solution.py
+++ b/solution.py
@@ -150,6 +150,13 @@
         inside[:, cols(h)] = split_dot(near, v_lin[:, cols(h)])
     vt[0] = v_soft[...].T
 
+    k_send[0].wait_recv()
+    k_pass = remote(k_in.at[0], k_in.at[2], k_ss.at[2], k_rs.at[2], seq=chips[2])
+    k_pass.start()
+    v_send[1].wait_recv()
+    v_pass = remote(v_in.at[1], v_in.at[2], v_ss.at[2], v_rs.at[2], seq=chips[1])
+    v_pass.start()
+
     for copy in s_send + d_send:
         copy.wait_recv()
     spans = [d_own[...]] + [d_in[r] for r in range(PLANE - 1)]
@@ -183,13 +190,6 @@
         def _(k=k):
             for copy in total_copies(k):
                 copy.start()
-
-    k_send[0].wait_recv()
-    k_pass = remote(k_in.at[0], k_in.at[2], k_ss.at[2], k_rs.at[2], seq=chips[2])
-    k_pass.start()
-    v_send[1].wait_recv()
-    v_pass = remote(v_in.at[1], v_in.at[2], v_ss.at[2], v_rs.at[2], seq=chips[1])
-    v_pass.start()
 
     scale = factor * math.log2(math.e)
 
@@ -404,6 +404,48 @@
                     copy.wait_send()
     for copy in out_copies:
         copy.wait()
+
+
+def deliver_kernel(lin, soft, lin_out, soft_out, held, in_sem, out_sem):
+    chunks = held.shape[1]
+    rows = held.shape[2]
+    fetch, store = [], []
+    for layer, (src, dst) in enumerate(((lin, lin_out), (soft, soft_out))):
+        for c in range(chunks):
+            piece = pl.ds(c * rows, rows)
+            fetch.append(
+                pltpu.make_async_copy(src.at[piece], held.at[layer, c], in_sem.at[layer, c])
+            )
+            store.append(
+                pltpu.make_async_copy(held.at[layer, c], dst.at[piece], out_sem.at[layer, c])
+            )
+    for copy in fetch:
+        copy.start()
+    for arrived, copy in zip(fetch, store):
+        arrived.wait()
+        copy.start()
+    for copy in store:
+        copy.wait()
+
+
+def deliver(lin, soft):
+    rows, columns = lin.shape
+    chunks = 4
+    anywhere = pl.BlockSpec(memory_space=pl.ANY)
+    out = jax.ShapeDtypeStruct(lin.shape, lin.dtype)
+    return pl.pallas_call(
+        deliver_kernel,
+        out_shape=(out, out),
+        in_specs=[anywhere] * 2,
+        out_specs=(anywhere, anywhere),
+        scratch_shapes=[
+            pltpu.VMEM((2, chunks, rows // chunks, columns), BF16),
+            pltpu.SemaphoreType.DMA((2, chunks)),
+            pltpu.SemaphoreType.DMA((2, chunks)),
+        ],
+        compiler_params=pltpu.CompilerParams(vmem_limit_bytes=60 * 1024 * 1024),
+        name="deliver",
+    )(lin, soft)
 
 
 def local(planes, groups, *arrays):
@@ -459,7 +501,7 @@
     scratch += [dma((2,)), dma((2, columns // min(columns, 512))), dma((7,))]
     anywhere = pl.BlockSpec(memory_space=pl.ANY)
     out = jax.ShapeDtypeStruct((rows, columns), BF16)
-    return pl.pallas_call(
+    results = pl.pallas_call(
         functools.partial(kernel, planes, groups, heads, 1.0 / math.sqrt(width)),
         out_shape=(out, out),
         in_specs=[anywhere] * 9,
@@ -470,6 +512,7 @@
         ),
         name="attention_layers",
     )(*arrays)
+    return deliver(*results)
 
 
 def solution(mesh):

time: 38.8 us -> 38.7 us (level)
  local copies, waits for them, and re-layouts: 3.37 us -> 0 us
  Pallas kernels: 34.6 us -> 37.9 us
    unnamed x4 -> x0, local copies, waits for them, and re-layouts: 3.37 us -> none
    pallas_call x0 -> x1, Pallas kernels: none -> 2.4 us  [deliver(): pl.pallas_call(deliver_kernel, out_shape=(out, out), in_specs=[anywhere]...]
    pallas_call x1, Pallas kernels: 34.6 us -> 35.6 us  [local(): pl.pallas_call(functools.partial(kernel, planes, groups, heads, 1.0 / mat...]
where the time goes in v4:
time: 38.7 us; the launch traced here: 38.6 us
  Pallas kernels  37.9 us (98%)
  between operations  0.64 us (2%)
    pallas_call x1, Pallas kernels, local(): pl.pallas_call(functools.partial(kernel, planes, groups, heads, 1.0 / mat...  35.6 us
    pallas_call x1, Pallas kernels, deliver(): pl.pallas_call(deliver_kernel, out_shape=(out, out), in_specs=[anywhere]...  2.4 us

profile of v4, /device:TPU:25, one launch (start us, length us, event | category | flops | bytes accessed | tf_op | source)
XLA Modules:
  0.0 38.6 jit_solution(11742344079716141089)
XLA Ops:
  0.6 35.6 %attention_layers.1 = (bf16[256,2048]{1,0:T(8,128)(2,1)}, bf16[256,2048]{1,0:T(8,128)(2,1)}) custom-call(bf16[256,256]{1,0:T(8,128)(2,1)} %q_lin_hbm.1, bf16[256,256]{1,0:T(8,128)(2,1)} %k_lin_hbm.1, bf16[256,256]{1,0:T(8,128)(2,1)} %v_lin_hbm.1, f32[2,256]{1,0:T(2,128)} %decay_hbm.1, bf16[256,256]{1,0:T(8,128)(2,1)} %q_hbm.1, bf16[256,256]{1,0:T(8,128)(2,1)} %k_hbm.1, ...), custom_call_target="tpu_custom_call" | custom-call | tf_op jit(solution)/shard_map/attention_layers/pallas_call | solution.py:504
  36.2 2.4 %deliver.1 = (bf16[256,2048]{1,0:T(8,128)(2,1)}, bf16[256,2048]{1,0:T(8,128)(2,1)}) custom-call(bf16[256,2048]{1,0:T(8,128)(2,1)} %get-tuple-element.4.lin, bf16[256,2048]{1,0:T(8,128)(2,1)} %get-tuple-element.5.soft), custom_call_target="tpu_custom_call" | custom-call | tf_op jit(solution)/shard_map/deliver/pallas_call | solution.py:436

commit v5 on v4

--- a/solution.py
+++ b/solution.py
@@ -150,13 +150,6 @@
         inside[:, cols(h)] = split_dot(near, v_lin[:, cols(h)])
     vt[0] = v_soft[...].T
 
-    k_send[0].wait_recv()
-    k_pass = remote(k_in.at[0], k_in.at[2], k_ss.at[2], k_rs.at[2], seq=chips[2])
-    k_pass.start()
-    v_send[1].wait_recv()
-    v_pass = remote(v_in.at[1], v_in.at[2], v_ss.at[2], v_rs.at[2], seq=chips[1])
-    v_pass.start()
-
     for copy in s_send + d_send:
         copy.wait_recv()
     spans = [d_own[...]] + [d_in[r] for r in range(PLANE - 1)]
@@ -190,6 +183,13 @@
         def _(k=k):
             for copy in total_copies(k):
                 copy.start()
+
+    k_send[0].wait_recv()
+    k_pass = remote(k_in.at[0], k_in.at[2], k_ss.at[2], k_rs.at[2], seq=chips[2])
+    k_pass.start()
+    v_send[1].wait_recv()
+    v_pass = remote(v_in.at[1], v_in.at[2], v_ss.at[2], v_rs.at[2], seq=chips[1])
+    v_pass.start()
 
     scale = factor * math.log2(math.e)
 

time: 38.7 us -> 37.8 us (0.977)
  Pallas kernels: 37.9 us -> 37 us
    pallas_call x1, Pallas kernels: 35.6 us -> 34.6 us  [local(): pl.pallas_call(functools.partial(kernel, planes, groups, heads, 1.0 / mat...]
where the time goes in v5:
time: 37.8 us; the launch traced here: 37.7 us
  Pallas kernels  37 us (98%)
  between operations  0.64 us (2%)
    pallas_call x1, Pallas kernels, local(): pl.pallas_call(functools.partial(kernel, planes, groups, heads, 1.0 / mat...  34.6 us
    pallas_call x1, Pallas kernels, deliver(): pl.pallas_call(deliver_kernel, out_shape=(out, out), in_specs=[anywhere]...  2.4 us

profile of v5, /device:TPU:25, one launch (start us, length us, event | category | flops | bytes accessed | tf_op | source)
XLA Modules:
  0.0 37.7 jit_solution(5642041482308636599)
XLA Ops:
  0.6 34.6 %attention_layers.1 = (bf16[256,2048]{1,0:T(8,128)(2,1)}, bf16[256,2048]{1,0:T(8,128)(2,1)}) custom-call(bf16[256,256]{1,0:T(8,128)(2,1)} %q_lin_hbm.1, bf16[256,256]{1,0:T(8,128)(2,1)} %k_lin_hbm.1, bf16[256,256]{1,0:T(8,128)(2,1)} %v_lin_hbm.1, f32[2,256]{1,0:T(2,128)} %decay_hbm.1, bf16[256,256]{1,0:T(8,128)(2,1)} %q_hbm.1, bf16[256,256]{1,0:T(8,128)(2,1)} %k_hbm.1, ...), custom_call_target="tpu_custom_call" | custom-call | tf_op jit(solution)/shard_map/attention_layers/pallas_call | solution.py:504
  35.3 2.4 %deliver.1 = (bf16[256,2048]{1,0:T(8,128)(2,1)}, bf16[256,2048]{1,0:T(8,128)(2,1)}) custom-call(bf16[256,2048]{1,0:T(8,128)(2,1)} %get-tuple-element.4.lin, bf16[256,2048]{1,0:T(8,128)(2,1)} %get-tuple-element.5.soft), custom_call_target="tpu_custom_call" | custom-call | tf_op jit(solution)/shard_map/deliver/pallas_call | solution.py:436
